TPU v7x, 128 devices: a whole 4x4x4 slice. The times are simulated.
128 devices in a mesh: seq: 8 (over x, core), head: 16 (over z, y).
Axes of the slice: x: 4, y: 4, z: 4, core: 2. Of those that a mesh axis runs over, the one named last changes fastest.
Arguments:
- tokens: bfloat16 [1024, 6144], P('seq'), may hold values from -6 to 6
- log_decay: float32 [1024, 32], P('seq', 'head'), may hold values from -1 to 0
- carried_state: float32 [32, 128, 128], P('head'), may hold values from -48 to 48
- q_weight: bfloat16 [6144, 4096], P(None, 'head'), may hold values from -0.078125 to 0.078125
- k_weight: bfloat16 [6144, 4096], P(None, 'head'), may hold values from -0.078125 to 0.078125
- v_weight: bfloat16 [6144, 4096], P(None, 'head'), may hold values from -0.078125 to 0.078125
- out_weight: bfloat16 [4096, 6144], P('head'), may hold values from -0.09375 to 0.09375
- final_gain: bfloat16 [6144], replicated, may hold values from 0.099609375 to 1.8984375
- vocab_weight: bfloat16 [6144, 131072], P(None, ('seq', 'head')), may hold values from -5 to 5
- targets: int32 [1024], replicated, may hold values from 0 to 131071
Outputs:
- loglik: float32 [1024], P('seq')
All inputs are finite; a program needn't handle non-finite values.
Results may differ from a plain program's by a relative error of at most 0.002.
Values may be sent and summed in bfloat16 or wider, within the bound.
No kernel may reach another device: no remote copies, remote signals or barrier semaphores. Data moves between devices by JAX's collectives and lax.ppermute only.
A program may use at most 128 MiB of HBM per device.

v0:
```python
import jax
import jax.numpy as jnp
from jax import lax
from jax.sharding import PartitionSpec as P


def prefix(array, axis, combine, identity):
    length, here = (lax.axis_size(axis), lax.axis_index(axis))
    everything = jax.tree.map(lambda part: lax.all_gather(part, axis), array)
    start = jax.tree.map(
        lambda part, zero: jnp.broadcast_to(jnp.asarray(zero, part.dtype), part.shape),
        array,
        identity,
    )

    def turn(k, before):
        reached = k < here
        new = combine(before, jax.tree.map(lambda part: part[k], everything))
        return jax.tree.map(lambda a, b: jnp.where(reached, a, b), new, before)

    return lax.fori_loop(0, length, turn, start)


def combine_states(earlier, later):
    return (earlier[0] * later[0], later[0][:, None, None] * earlier[1] + later[1])


def shards(
    tokens,
    log_decay,
    carried_state,
    q_weight,
    k_weight,
    v_weight,
    out_weight,
    final_gain,
    vocab_weight,
    targets,
):
    highest = lax.Precision.HIGHEST
    rows_here = tokens.shape[0]
    heads_here = carried_state.shape[0]
    head_size = carried_state.shape[1]
    view = (rows_here, heads_here, head_size)
    queries = (
        jnp.dot(tokens, q_weight, preferred_element_type=jnp.float32)
        .astype(jnp.bfloat16)
        .reshape(view)
    )
    keys_loc = (
        jnp.dot(tokens, k_weight, preferred_element_type=jnp.float32)
        .astype(jnp.bfloat16)
        .reshape(view)
    )
    values = (
        jnp.dot(tokens, v_weight, preferred_element_type=jnp.float32)
        .astype(jnp.bfloat16)
        .reshape(view)
    )
    cumul = jnp.cumsum(log_decay, axis=0)
    last_cum = cumul[-1]
    ends = jnp.exp(last_cum[None, :] - cumul)
    local_state = jnp.einsum(
        "thd,the->hde",
        keys_loc.astype(jnp.float32) * ends[:, :, None],
        values.astype(jnp.float32),
        precision=highest,
    )
    total_decay = jnp.exp(last_cum)
    prefix_decay, prefix_state = prefix(
        (total_decay, local_state),
        "seq",
        combine_states,
        (jnp.ones_like(total_decay), jnp.zeros_like(local_state)),
    )
    lower = jnp.arange(rows_here)[:, None] >= jnp.arange(rows_here)[None, :]
    scores = jnp.einsum("thd,shd->hts", queries, keys_loc, preferred_element_type=jnp.float32)
    diff = jnp.transpose(cumul[:, None, :] - cumul[None, :, :], (2, 0, 1))
    weight = (scores * jnp.exp(jnp.where(lower[None], diff, -1e30))).astype(jnp.bfloat16)
    intra = jnp.einsum("hts,shd->thd", weight, values, preferred_element_type=jnp.float32)
    state_in = prefix_decay[:, None, None] * carried_state + prefix_state
    inter = jnp.exp(cumul)[:, :, None] * jnp.einsum(
        "thd,hde->the", queries.astype(jnp.float32), state_in, precision=highest
    )
    attended = intra + inter
    normed_heads = attended * lax.rsqrt(
        jnp.mean(attended * attended, axis=-1, keepdims=True) + 1e-06
    )
    flat_heads = normed_heads.astype(jnp.bfloat16).reshape(rows_here, heads_here * head_size)
    rows_mine = rows_here // lax.axis_size("head")
    head_index = lax.axis_index("head")
    mixed_all = lax.psum(
        jnp.dot(flat_heads, out_weight, preferred_element_type=jnp.float32), "head"
    )
    mixed = lax.dynamic_slice_in_dim(mixed_all, head_index * rows_mine, rows_mine, 0)
    resid = (
        lax.dynamic_slice_in_dim(tokens, head_index * rows_mine, rows_mine, 0).astype(jnp.float32)
        + mixed
    )
    final_rows = (
        resid
        * lax.rsqrt(jnp.mean(resid * resid, axis=-1, keepdims=True) + 1e-06)
        * final_gain.astype(jnp.float32)
    )
    final_rows = final_rows.astype(jnp.bfloat16)
    vocab_local = vocab_weight.shape[1]
    offset = (lax.axis_index("seq") * lax.axis_size("head") + head_index) * vocab_local
    columns = jnp.arange(vocab_local, dtype=jnp.int32)
    logits = jnp.dot(
        lax.all_gather(final_rows, ("seq", "head"), axis=0, tiled=True),
        vocab_weight,
        preferred_element_type=jnp.float32,
    )
    top = jnp.max(logits, axis=1)
    total = jnp.sum(jnp.exp(logits - top[:, None]), axis=1)
    wanted = targets - offset
    hit = jnp.sum(jnp.where(columns[None, :] == wanted[:, None], logits, 0.0), axis=1)
    top_all = lax.pmax(top, ("seq", "head"))
    total_all, hit_all = lax.psum((total * jnp.exp(top - top_all), hit), ("seq", "head"))
    loglik = hit_all - top_all - jnp.log(total_all)
    return lax.dynamic_slice_in_dim(loglik, lax.axis_index("seq") * rows_here, rows_here, 0)


def solution(mesh):
    return jax.shard_map(
        shards,
        mesh=mesh,
        in_specs=(
            P("seq", None),
            P("seq", "head"),
            P("head", None, None),
            P(None, "head"),
            P(None, "head"),
            P(None, "head"),
            P("head", None),
            P(),
            P(None, ("seq", "head")),
            P(),
        ),
        out_specs=P("seq"),
        check_vma=False,
    )
```

profile of v0, /device:TPU:1, one launch (start us, length us, event | category | flops | bytes accessed | tf_op | source)
XLA Modules:
  0.0 385.3 jit_solution(14718534888018662489)
XLA Ops:
  6.5 0.0 copy-start
  6.5 0.0 all-gather.7.cloned.1.call-start
  6.5 0.9 copy.23
  7.5 0.2 reduce_window_sum.11
  7.7 0.1 copy.30
  7.7 3.0 convolution_convert_fusion
  10.7 0.1 copy.36
  10.8 3.0 fusion.4
  13.8 0.9 fusion.8
  14.6 0.0 all-gather.7.cloned.1.call-update
  14.7 0.0 all-reduce.3.cloned.1.call-start
  14.7 11.8 %all-gather.1 = f32[8,1,2]{2,1,0:T(1,128)S(1)} all-gather(f32[1,1,2]{2,1,0:T(1,128)S(1)} %get-tuple-element.171), channel_id=1, replica_groups=mesh['seq'=8,'head'=16] {'seq'}, dimensions={0}, use_global_device_ids=true | all-gather | bytes 72 | tf_op jit(solution)/shard_map/all_gather | solution.py:9
  26.5 0.1 copy.27
  26.6 0.1 copy.24
  26.7 3.1 fusion.5
  29.8 12.0 %all-gather.7.cloned.1.call-done = f32[16,128,128]{2,1,0:T(8,128)} async-done(((f32[2,128,128]{2,1,0:T(8,128)}), f32[16,128,128]{2,1,0:T(8,128)}) %all-gather.7.cloned.1.call-update) | async-done | bytes 1048592 | tf_op jit(solution)/shard_map/all_gather | solution.py:9
  41.8 8.3 %while.16 = (s32[]{:T(128)}, f32[2]{0:T(128)S(1)}, f32[2,128,128]{2,1,0:T(8,128)S(1)}, s32[]{:T(128)}, f32[8,2]{1,0:T(8,128)S(1)}, /*index=5*/f32[8,2,128,128]{3,2,1,0:T(8,128)}, s32[]{:T(128)}, s32[]{:T(128)}) while((s32[]{:T(128)}, f32[2]{0:T(128)S(1)}, f32[2,128,128]{2,1,0:T(8,128)S(1)}, s32[]{:T(128)}, f32[8,2]{1,0:T(8,128)S(1)}, ...), condition=%wide.region_2.3_spmd.clone, body=%wide.region_1.2_spmd.clone.sunk | while | flops 131082 | bytes 393371 | solution.py:21
  41.8 1.0 fusion.48
  42.8 1.0 fusion.48
  43.9 1.0 fusion.48
  44.9 1.0 fusion.48
  46.0 1.0 fusion.48
  47.0 1.0 fusion.48
  48.0 1.0 fusion.48
  49.1 1.0 fusion.48
  50.1 1.9 fusion.1
  52.0 1.2 multiply_reduce_fusion.1
  53.3 0.0 copy-done
  53.3 2.3 fusion.35
  55.6 0.0 copy-start.1
  55.6 0.0 copy-start.2
  55.6 0.0 all-reduce.3.cloned.1.call-update
  55.6 0.0 all-gather.5.cloned.1.call-start
  55.7 0.6 copy-done.1
  56.3 94.3 %all-reduce.3.cloned.1.call-done = f32[128,6144]{1,0:T(8,128)} async-done(((f32[128,6144]{1,0:T(8,128)}), f32[128,6144]{1,0:T(8,128)}) %all-reduce.3.cloned.1.call-update) | async-done | bytes 3145744 | tf_op jit(solution)/shard_map/psum | solution.py:92
  150.6 1.2 multiply_reduce_fusion
  151.8 1.7 multiply_convert_fusion
  153.5 0.0 all-gather.5.cloned.1.call-update
  153.5 0.0 copy-done.2
  153.6 73.3 %all-gather.5.cloned.1.call-done = bf16[1024,6144]{1,0:T(8,128)(2,1)} async-done(((bf16[8,6144]{1,0:T(8,128)(2,1)}), bf16[1024,6144]{1,0:T(8,128)(2,1)}) %all-gather.5.cloned.1.call-update) | async-done | bytes 12582928 | tf_op jit(solution)/shard_map/all_gather | solution.py:110
  226.9 19.4 %fusion.34 = (f32[1024]{0:T(1024)S(1)}, f32[1024,1024]{0,1:T(8,128)}) fusion(bf16[1024,6144]{1,0:T(8,128)(2,1)} %all-gather.5.cloned.1.call-done, bf16[6144,1024]{1,0:T(8,128)(2,1)} %param.20), kind=kOutput, calls=%fused_computation.57 | convolution fusion | flops 12885949440 | bytes 29364224 | tf_op jit(solution)/shard_map/dot_general | solution.py:109
  246.3 64.4 %pmax.7 = f32[1024]{0:T(1024)S(1)} all-reduce(f32[1024]{0:T(1024)S(1)} %get-tuple-element.174), channel_id=1, replica_groups=mesh['seq'=8,'head'=16] {'seq','head'}, use_global_device_ids=true, to_apply=%region_9.10 | all-reduce | flops 1024 | bytes 8192 | tf_op jit(solution)/shard_map/pmax | solution.py:118
  310.7 3.3 select_reduce_fusion
  314.0 64.2 %all-reduce = (f32[1024]{0:T(1024)S(1)}, f32[1024]{0:T(1024)S(1)}) all-reduce(f32[1024]{0:T(1024)S(1)} %exponential_multiply_fusion, f32[1024]{0:T(1024)S(1)} %get-tuple-element.150), channel_id=1, replica_groups=mesh['seq'=8,'head'=16] {'seq','head'}, use_global_device_ids=true, to_apply=%region_11.12 | all-reduce | flops 2048 | bytes 16384 | tf_op jit(solution)/shard_map/psum | solution.py:119
  378.2 0.6 dynamic_slice.25
  (20 shorter events, 0.3 us)
Async XLA Ops:
  6.5 46.7 %copy-start = (bf16[256,6144]{1,0:T(8,128)(2,1)S(1)}, bf16[256,6144]{1,0:T(8,128)(2,1)}, u32[]{:S(2)}) copy-start(bf16[256,6144]{1,0:T(8,128)(2,1)} %param.18) | copy-start | bytes 9437188
  6.5 35.2 %all-gather.7.cloned.1.call-start = ((), (), s32[]{:S(2)}) async-start(), calls=%async_computation.2 | async-start | bytes 1179648 | tf_op jit(solution)/shard_map/all_gather | solution.py:9
  14.7 135.9 %all-reduce.3.cloned.1.call-start = ((), (), s32[]{:S(2)}) async-start(), calls=%async_computation | async-start | bytes 6291456 | tf_op jit(solution)/shard_map/psum | solution.py:92
  55.6 0.7 copy-start.1
  55.6 98.0 %copy-start.2 = (s32[1024]{0:T(1024)S(1)}, s32[1024]{0:T(1024)}, u32[]{:S(2)}) copy-start(s32[1024]{0:T(1024)} %param.21) | copy-start | bytes 12292
  55.6 171.3 %all-gather.5.cloned.1.call-start = ((), (), s32[]{:S(2)}) async-start(), calls=%async_computation.1 | async-start | bytes 12681216 | tf_op jit(solution)/shard_map/all_gather | solution.py:110
Sparse Core Ops, SparseCore 0:
  14.8 26.9 all-gather.6
  55.7 94.8 all-reduce.2
  153.7 73.0 all-gather.4
where the time goes:
time: 386 us; the launch traced here: 385 us
  waiting for transfers between devices  180 us (47%)
  blocking collectives  140 us (36%)
  matrix products  34.7 us (9%)
  other arithmetic  14.5 us (4%)
  between operations  13.2 us (3%)
    psum x1, waiting for transfers between devices, shards(): lax.psum(jnp.dot(flat_heads, out_weight, preferred_element_type=jnp.float...  94.3 us
    all_gather x1, waiting for transfers between devices, shards(): lax.all_gather(final_rows, ('seq', 'head'), axis=0, tiled=True)  73.3 us
    pmax x1, blocking collectives, shards(): top_all = lax.pmax(top, ('seq', 'head'))  64.4 us
    psum x1, blocking collectives, shards(): lax.psum((total * jnp.exp(top - top_all), hit), ('seq', 'head'))  64.2 us
    dot_general x1, matrix products, shards(): jnp.dot(lax.all_gather(final_rows, ('seq', 'head'), axis=0, tiled=True),...  19.4 us
    all_gather x1, waiting for transfers between devices, prefix(): everything = jax.tree.map(lambda part: lax.all_gather(part, axis), array)  12 us
    all_gather x1, blocking collectives, prefix(): everything = jax.tree.map(lambda part: lax.all_gather(part, axis), array)  11.8 us
    select_n x16, other arithmetic, turn(): return jax.tree.map(lambda a, b: jnp.where(reached, a, b), new, before)  8.09 us
  transfers between devices with their start and end apart: 3, of which 3 were waited for; matrix products, arithmetic and copies ran while one was open for 1% of the time, Pallas kernels for 0%

commit v1 on v0

--- a/solution.py
+++ b/solution.py
@@ -89,9 +89,11 @@
     flat_heads = normed_heads.astype(jnp.bfloat16).reshape(rows_here, heads_here * head_size)
     rows_mine = rows_here // lax.axis_size("head")
     head_index = lax.axis_index("head")
-    mixed_all = lax.psum(
-        jnp.dot(flat_heads, out_weight, preferred_element_type=jnp.float32), "head"
-    )
+
+    def _answer_zones(page):
+        return jnp.sum(lax.all_gather(page, "head"), 0)
+
+    mixed_all = _answer_zones(jnp.dot(flat_heads, out_weight, preferred_element_type=jnp.float32))
     mixed = lax.dynamic_slice_in_dim(mixed_all, head_index * rows_mine, rows_mine, 0)
     resid = (
         lax.dynamic_slice_in_dim(tokens, head_index * rows_mine, rows_mine, 0).astype(jnp.float32)

time: 386 us -> 591 us (1.53)
  waiting for transfers between devices: 180 us -> 367 us
  other arithmetic: 14.5 us -> 31.6 us
    all_gather x0 -> x1, waiting for transfers between devices: none -> 282 us  [_answer_zones(): return jnp.sum(lax.all_gather(page, 'head'), 0)]
    psum x1 -> x0, waiting for transfers between devices: 94.3 us -> none  [shards(): lax.psum(jnp.dot(flat_heads, out_weight, preferred_element_type=jnp.float...]
    reduce_sum x0 -> x1, other arithmetic: none -> 17.3 us  [_answer_zones(): return jnp.sum(lax.all_gather(page, 'head'), 0)]
where the time goes in v1:
time: 591 us; the launch traced here: 590 us
  waiting for transfers between devices  367 us (62%)
  blocking collectives  140 us (24%)
  matrix products  34.7 us (6%)
  other arithmetic  31.6 us (5%)
  between operations  13.2 us (2%)
    all_gather x1, waiting for transfers between devices, _answer_zones(): return jnp.sum(lax.all_gather(page, 'head'), 0)  282 us
    all_gather x1, waiting for transfers between devices, shards(): lax.all_gather(final_rows, ('seq', 'head'), axis=0, tiled=True)  73.5 us
    pmax x1, blocking collectives, shards(): top_all = lax.pmax(top, ('seq', 'head'))  64.4 us
    psum x1, blocking collectives, shards(): lax.psum((total * jnp.exp(top - top_all), hit), ('seq', 'head'))  64.2 us
    dot_general x1, matrix products, shards(): jnp.dot(lax.all_gather(final_rows, ('seq', 'head'), axis=0, tiled=True),...  19.5 us
    reduce_sum x1, other arithmetic, _answer_zones(): return jnp.sum(lax.all_gather(page, 'head'), 0)  17.3 us
    all_gather x1, waiting for transfers between devices, prefix(): everything = jax.tree.map(lambda part: lax.all_gather(part, axis), array)  12 us
    all_gather x1, blocking collectives, prefix(): everything = jax.tree.map(lambda part: lax.all_gather(part, axis), array)  11.8 us
  transfers between devices with their start and end apart: 3, of which 3 were waited for; matrix products, arithmetic and copies ran while one was open for 1% of the time, Pallas kernels for 0%

profile of v1, /device:TPU:1, one launch (start us, length us, event | category | flops | bytes accessed | tf_op | source)
XLA Modules:
  0.0 590.2 jit_solution(7105345002370355773)
XLA Ops:
  6.5 0.0 copy-start
  6.5 0.0 all-gather.9.cloned.1.call-start
  6.5 0.9 copy.23
  7.5 0.2 reduce_window_sum.11
  7.7 0.1 copy.30
  7.7 3.0 convolution_convert_fusion
  10.7 0.1 copy.36
  10.8 3.0 fusion.4
  13.8 0.9 fusion.8
  14.6 0.0 all-gather.9.cloned.1.call-update
  14.7 0.0 all-gather.11.cloned.1.call-start
  14.7 11.8 %all-gather.2 = f32[8,1,2]{2,1,0:T(1,128)S(1)} all-gather(f32[1,1,2]{2,1,0:T(1,128)S(1)} %get-tuple-element.171), channel_id=1, replica_groups=mesh['seq'=8,'head'=16] {'seq'}, dimensions={0}, use_global_device_ids=true | all-gather | bytes 72 | tf_op jit(solution)/shard_map/all_gather | solution.py:9
  26.5 0.1 copy.27
  26.6 0.1 copy.24
  26.7 3.1 fusion.5
  29.8 12.0 %all-gather.9.cloned.1.call-done = f32[16,128,128]{2,1,0:T(8,128)} async-done(((f32[2,128,128]{2,1,0:T(8,128)}), f32[16,128,128]{2,1,0:T(8,128)}) %all-gather.9.cloned.1.call-update) | async-done | bytes 1048592 | tf_op jit(solution)/shard_map/all_gather | solution.py:9
  41.8 8.3 %while.16 = (s32[]{:T(128)}, f32[2]{0:T(128)S(1)}, f32[2,128,128]{2,1,0:T(8,128)S(1)}, s32[]{:T(128)}, f32[8,2]{1,0:T(8,128)S(1)}, /*index=5*/f32[8,2,128,128]{3,2,1,0:T(8,128)}, s32[]{:T(128)}, s32[]{:T(128)}) while((s32[]{:T(128)}, f32[2]{0:T(128)S(1)}, f32[2,128,128]{2,1,0:T(8,128)S(1)}, s32[]{:T(128)}, f32[8,2]{1,0:T(8,128)S(1)}, ...), condition=%wide.region_2.3_spmd.clone, body=%wide.region_1.2_spmd.clone.sunk | while | flops 131082 | bytes 393371 | solution.py:21
  41.8 1.0 fusion.48
  42.8 1.0 fusion.48
  43.9 1.0 fusion.48
  44.9 1.0 fusion.48
  46.0 1.0 fusion.48
  47.0 1.0 fusion.48
  48.0 1.0 fusion.48
  49.1 1.0 fusion.48
  50.1 1.9 fusion.1
  52.0 1.2 multiply_reduce_fusion.1
  53.3 0.0 copy-done
  53.3 2.2 fusion.35
  55.5 0.0 copy-start.2
  55.5 0.0 all-gather.11.cloned.1.call-update
  55.5 0.0 all-gather.7.cloned.1.call-start
  55.6 0.6 copy-done.2
  56.2 281.9 %all-gather.11.cloned.1.call-done = f32[2048,6144]{1,0:T(8,128)} async-done(((f32[128,6144]{1,0:T(8,128)}), f32[2048,6144]{1,0:T(8,128)}) %all-gather.11.cloned.1.call-update) | async-done | bytes 50331664 | tf_op jit(solution)/shard_map/all_gather | solution.py:94
  338.1 0.0 copy-start.3
  338.1 17.3 %reduce_sum.46 = f32[128,6144]{1,0:T(8,128)S(1)} reduce(f32[16,128,6144]{2,1,0:T(8,128)} %bitcast.57, f32[]{:T(128)} %constant.55.clone.1), dimensions={0}, to_apply=%region_4.5 | reduce | flops 11796480 | bytes 53477380 | tf_op jit(solution)/shard_map/reduce_sum | solution.py:94
  355.4 1.1 multiply_reduce_fusion
  356.5 1.6 multiply_convert_fusion
  358.1 0.0 all-gather.7.cloned.1.call-update
  358.1 0.0 copy-done.3
  358.1 73.5 %all-gather.7.cloned.1.call-done = bf16[1024,6144]{1,0:T(8,128)(2,1)} async-done(((bf16[8,6144]{1,0:T(8,128)(2,1)}), bf16[1024,6144]{1,0:T(8,128)(2,1)}) %all-gather.7.cloned.1.call-update) | async-done | bytes 12582928 | tf_op jit(solution)/shard_map/all_gather | solution.py:112
  431.6 0.0 copy-start.1
  431.6 19.5 %fusion.34 = (f32[1024]{0:T(1024)S(1)}, f32[1024,1024]{0,1:T(8,128)}) fusion(bf16[1024,6144]{1,0:T(8,128)(2,1)} %all-gather.7.cloned.1.call-done, bf16[6144,1024]{1,0:T(8,128)(2,1)} %param.20), kind=kOutput, calls=%fused_computation.57 | convolution fusion | flops 12885949440 | bytes 29364224 | tf_op jit(solution)/shard_map/dot_general | solution.py:111
  451.1 64.4 %pmax.7 = f32[1024]{0:T(1024)S(1)} all-reduce(f32[1024]{0:T(1024)S(1)} %get-tuple-element.174), channel_id=1, replica_groups=mesh['seq'=8,'head'=16] {'seq','head'}, use_global_device_ids=true, to_apply=%region_9.10 | all-reduce | flops 1024 | bytes 8192 | tf_op jit(solution)/shard_map/pmax | solution.py:120
  515.5 3.3 select_reduce_fusion
  518.9 64.2 %all-reduce = (f32[1024]{0:T(1024)S(1)}, f32[1024]{0:T(1024)S(1)}) all-reduce(f32[1024]{0:T(1024)S(1)} %exponential_multiply_fusion, f32[1024]{0:T(1024)S(1)} %get-tuple-element.150), channel_id=1, replica_groups=mesh['seq'=8,'head'=16] {'seq','head'}, use_global_device_ids=true, to_apply=%region_11.12 | all-reduce | flops 2048 | bytes 16384 | tf_op jit(solution)/shard_map/psum | solution.py:121
  583.1 0.6 dynamic_slice.25
  583.7 0.0 copy-done.1
  (20 shorter events, 0.3 us)
Async XLA Ops:
  6.5 46.7 %copy-start = (bf16[256,6144]{1,0:T(8,128)(2,1)S(1)}, bf16[256,6144]{1,0:T(8,128)(2,1)}, u32[]{:S(2)}) copy-start(bf16[256,6144]{1,0:T(8,128)(2,1)} %param.18) | copy-start | bytes 9437188
  6.5 35.2 %all-gather.9.cloned.1.call-start = ((), (), s32[]{:S(2)}) async-start(), calls=%async_computation.1 | async-start | bytes 1179648 | tf_op jit(solution)/shard_map/all_gather | solution.py:9
  14.7 323.4 %all-gather.11.cloned.1.call-start = ((), (), s32[]{:S(2)}) async-start(), calls=%async_computation.2 | async-start | bytes 53477376 | tf_op jit(solution)/shard_map/all_gather | solution.py:94
  55.5 0.7 copy-start.2
  55.5 376.1 %all-gather.7.cloned.1.call-start = ((), (), s32[]{:S(2)}) async-start(), calls=%async_computation | async-start | bytes 12681216 | tf_op jit(solution)/shard_map/all_gather | solution.py:112
  338.1 20.0 %copy-start.3 = (s32[1024]{0:T(1024)S(1)}, s32[1024]{0:T(1024)}, u32[]{:S(2)}) copy-start(s32[1024]{0:T(1024)} %param.21) | copy-start | bytes 12292
  431.6 152.1 %copy-start.1 = (bf16[256,6144]{1,0:T(8,128)(2,1)S(1)}, bf16[256,6144]{1,0:T(8,128)(2,1)}, u32[]{:S(2)}) copy-start(bf16[256,6144]{1,0:T(8,128)(2,1)} %param.18) | copy-start | bytes 9437188
Sparse Core Ops, SparseCore 0:
  14.8 26.9 all-gather.8
  55.6 282.4 all-gather.10
  358.2 73.3 all-gather.6
